TPU v7x, 512 devices: a whole 4x8x8 slice. The times are simulated.
512 devices in a mesh: clu: 32 (over x, z), bank: 16 (over y, core).
Axes of the slice: x: 4, y: 8, z: 8, core: 2. Of those that a mesh axis runs over, the one named last changes fastest.
Arguments:
- queries: bfloat16 [131072, 3584], P(('clu', 'bank')), may hold values from -4 to 4
- bank: bfloat16 [32768, 3584], P(('clu', 'bank')), may hold values from -4 to 4
- cluster_ids: int32 [131072, 1], P(('clu', 'bank')), may hold values from 0 to 31; in each aligned block of 256 rows (0 to 255, 256 to 511, ...) at most 12 rows name the same one
- block_lists: int32 [131072, 8], P(('clu', 'bank')), may hold values from 0 to 15, all different within a row
- positive_ids: int32 [131072], P(('clu', 'bank')), may hold values from 0 to 1023
- loss_weights: float32 [131072], P(('clu', 'bank')), may hold values from 0.5 to 2
Outputs:
- query_grad: bfloat16 [131072, 3584], P(('clu', 'bank'))
- losses: bfloat16 [131072], P(('clu', 'bank'))
Inputs may be any that keep to these rules, and one draw needn't show every extreme that they name: `cluster_ids`: at most 12 of the 256 queries of one device name the same cluster. `block_lists`: each query lists 8 different blocks.
All inputs are finite; a program needn't handle non-finite values.
Results may differ from a plain program's by a relative error of at most 0.0051.
Values may be sent and summed in bfloat16 or wider, within the bound.
A program may use at most 64 MiB of HBM per device.

v0:
```python
import math

import jax
import jax.numpy as jnp
from jax import lax
from jax.sharding import PartitionSpec as P

D = 3584


def softmax_parts(logits, allowed, positive):
    usable = allowed > 0
    top = jnp.max(jnp.where(usable, logits, -jnp.inf), axis=1)
    total = jnp.sum(jnp.where(usable, jnp.exp(logits - top[:, None]), 0.0), axis=1)
    lse = top + jnp.log(total)
    pos_logit = jnp.take_along_axis(logits, positive[:, None], axis=1)[:, 0]
    probs = jnp.where(usable, jnp.exp(logits - lse[:, None]), 0.0).astype(jnp.bfloat16)
    return ((lse - pos_logit).astype(jnp.bfloat16), probs)


def cluster_work(arrived, arrived_labels, bank):
    blocks_count = lax.axis_size("bank")
    block_rows = bank.shape[0]
    listed = arrived_labels.shape[1] - 1
    scale = 3.0 / math.sqrt(D)
    lists = arrived_labels[:, :listed]
    positive = arrived_labels[:, listed]
    block_ids = jnp.arange(blocks_count, dtype=jnp.int32)
    block_mask = jnp.any(lists[:, :, None] == block_ids[None, None, :], axis=1)
    block_mask = block_mask | ((positive // block_rows)[:, None] == block_ids[None, :])
    allowed = jnp.repeat(block_mask, block_rows, axis=1).astype(jnp.int32)
    contract = (((1,), (1,)), ((), ()))
    logits = (
        lax.dot_general(
            arrived,
            lax.all_gather(bank, "bank", axis=0, tiled=True),
            contract,
            preferred_element_type=jnp.float32,
        )
        * scale
    )
    loss, probs = softmax_parts(logits, allowed, positive)
    piece = lax.all_gather(bank, "bank", axis=0, tiled=True)
    span = piece.shape[0]
    inside = (positive >= 0) & (positive < span)
    picked = jnp.take(piece, jnp.clip(positive, 0, span - 1), axis=0).astype(jnp.float32)
    product = jnp.dot(probs, piece, preferred_element_type=jnp.float32)
    pulled = product - jnp.where(inside[:, None], picked, 0.0)
    cached = (scale * pulled).astype(jnp.bfloat16)
    return (cached, loss)


def body(queries, bank, cluster_ids, block_lists, positive_ids, loss_weights):
    owners = lax.axis_size("clu")
    count = queries.shape[0]
    width = queries.shape[1]
    listed = block_lists.shape[1]
    capacity = max(2, 3 * count // (2 * owners))
    total_slots = owners * capacity
    target = cluster_ids[:, 0]
    onehot = (target[:, None] == jnp.arange(owners, dtype=jnp.int32)[None, :]).astype(jnp.int32)
    before = jnp.cumsum(onehot, axis=0) - onehot
    slot = target * capacity + jnp.sum(before * onehot, axis=1)
    outgoing = jnp.zeros((total_slots, width), jnp.bfloat16).at[slot].set(queries)
    labels = jnp.concatenate([block_lists, positive_ids[:, None]], axis=1)
    out_labels = jnp.zeros((total_slots, listed + 1), jnp.int32).at[slot].set(labels)
    out_rows = outgoing.reshape(owners, capacity, width)
    out_tags = out_labels.reshape(owners, capacity, listed + 1)
    arrived = lax.all_to_all(out_rows, "clu", split_axis=0, concat_axis=0, tiled=True).reshape(
        total_slots, width
    )
    arrived_labels = lax.all_to_all(
        out_tags, "clu", split_axis=0, concat_axis=0, tiled=True
    ).reshape(total_slots, listed + 1)
    cached, loss = cluster_work(arrived, arrived_labels, bank)
    back_grad, back_loss = (
        lax.all_to_all(
            cached.reshape(owners, capacity, width), "clu", split_axis=0, concat_axis=0, tiled=True
        ),
        lax.all_to_all(
            loss.reshape(owners, capacity), "clu", split_axis=0, concat_axis=0, tiled=True
        ),
    )
    mine_grad = back_grad.reshape(total_slots, width)[slot]
    mine_loss = back_loss.reshape(total_slots)[slot]
    query_grad = (loss_weights[:, None] * mine_grad.astype(jnp.float32)).astype(jnp.bfloat16)
    return (query_grad, mine_loss)


def solution(mesh):
    placed = (
        P(("clu", "bank"), None),
        P(("clu", "bank"), None),
        P(("clu", "bank"), None),
        P(("clu", "bank"), None),
        P(("clu", "bank")),
        P(("clu", "bank")),
    )
    return jax.shard_map(
        body,
        mesh=mesh,
        in_specs=placed,
        out_specs=(P(("clu", "bank"), None), P(("clu", "bank"))),
        check_vma=False,
    )
```

profile of v0, /device:TPU:1, one launch (start us, length us, event | category | flops | bytes accessed | tf_op | source)
XLA Modules:
  0.0 285.9 jit_solution(15249485596598394481)
XLA Ops:
  7.2 0.7 all-gather.2.cloned.1.call-update
  7.9 0.7 fusion.12
  8.6 0.6 reduce-window.6
  9.2 0.2 slice_reduce_fusion
  9.4 0.7 pad_add_fusion
  10.2 0.8 fusion.11
  11.0 0.7 compare_select_fusion.1
  11.7 1.2 scatter_custom_fusion
  13.0 0.2 reshape.119
  13.2 0.8 copy.28
  14.0 13.7 %all-to-all-start = ((s32[32,12,9]{1,2,0:T(8,128)}), s32[32,12,9]{1,2,0:T(8,128)S(1)}, u32[]{:S(2)}, u32[]{:S(2)}) async-start(s32[32,12,9]{1,2,0:T(8,128)} %copy.28), calls=%async_computation | async-start | bytes 524288 | tf_op jit(solution)/shard_map/all_to_all | solution.py:72
  27.7 4.9 %scatter_custom_fusion.1 = bf16[384,3584]{1,0:T(8,128)(2,1)S(1)} fusion(s32[256]{0:T(256)S(1)} %bitcast.40, bf16[256,3584]{1,0:T(8,128)(2,1)} %param.6, bf16[]{:T(256)} %constant.62.clone.1), kind=kCustom, calls=%fused_computation.14 | custom fusion | bytes 2753024 | tf_op jit(solution)/shard_map/scatter | solution.py:64
  32.6 2.5 reshape.121
  35.2 2.2 all-to-all-done
  37.4 7.1 %all-to-all-start.1 = ((bf16[32,12,3584]{2,1,0:T(8,128)(2,1)}), bf16[32,12,3584]{2,1,0:T(8,128)(2,1)}, u32[]{:S(2)}, u32[]{:S(2)}) async-start(bf16[32,12,3584]{2,1,0:T(8,128)(2,1)} %reshape.121), calls=%async_computation.1 | async-start | bytes 7340032 | tf_op jit(solution)/shard_map/all_to_all | solution.py:69
  44.9 0.5 copy.32
  45.5 84.4 %all-to-all-done.1 = bf16[32,12,3584]{2,1,0:T(8,128)(2,1)} async-done(((bf16[32,12,3584]{2,1,0:T(8,128)(2,1)}), bf16[32,12,3584]{2,1,0:T(8,128)(2,1)}, u32[]{:S(2)}, u32[]{:S(2)}) %all-to-all-start.1) | async-done | bytes 2752544 | tf_op jit(solution)/shard_map/all_to_all | solution.py:69
  129.9 5.4 %reshape.122 = bf16[384,3584]{1,0:T(8,128)(2,1)} reshape(bf16[32,12,3584]{2,1,0:T(8,128)(2,1)} %all-to-all-done.1) | data formatting | bytes 5505024 | tf_op jit(solution)/shard_map/reshape | solution.py:69
  135.3 6.3 %select_reduce_fusion.1 = (f32[384]{0:T(512)S(1)}, f32[384,1024]{1,0:T(8,128)S(1)}) fusion(pred[384,1024]{1,0:T(32,128)(4,1)S(1)} %copy.32, bf16[384,3584]{1,0:T(8,128)(2,1)} %reshape.122, bf16[1024,3584]{1,0:T(8,128)(2,1)} %all-gather.2.cloned.1.call-done), kind=kOutput, calls=%fused_computation.12 | convolution fusion | flops 2819751424 | bytes 12060160 | tf_op jit(solution)/shard_map/dot_general | solution.py:34
  141.7 0.5 select_reduce_fusion
  142.3 3.5 %gather_fusion.3 = f32[384]{0:T(512)S(1)} fusion(f32[384,1024]{1,0:T(8,128)S(1)} %get-tuple-element.8, s32[384]{0:T(512)S(1)} %fusion.18), kind=kCustom, calls=%fused_computation.3 | custom fusion | bytes 6144 | tf_op jit(solution)/shard_map/jit(take_along_axis)/gather | solution.py:16
  145.9 0.6 copy.33
  146.5 6.0 %all-to-all-start.3 = ((bf16[32,1,12]{2,1,0:T(2,128)(2,1)}), bf16[32,1,12]{2,1,0:T(2,128)(2,1)S(1)}, u32[]{:S(2)}, u32[]{:S(2)}) async-start(bf16[32,1,12]{2,1,0:T(2,128)(2,1)} %copy.33), calls=%async_computation.3 | async-start | bytes 32768 | tf_op jit(solution)/shard_map/all_to_all | solution.py:80
  152.5 11.6 %gather_fusion = bf16[384,3584]{1,0:T(8,128)(2,1)} fusion(bf16[1024,3584]{1,0:T(8,128)(2,1)} %all-gather.2.cloned.1.call-done, s32[1024]{0:T(1024)S(1)} %pad_clamp_fusion.1), kind=kCustom, calls=%fused_computation | custom fusion | bytes 5506560 | tf_op jit(solution)/shard_map/jit(_take)/gather | solution.py:46
  164.1 8.4 %fusion.1 = bf16[384,3584]{1,0:T(8,128)(2,1)} fusion(bf16[1024,3584]{1,0:T(8,128)(2,1)} %all-gather.2.cloned.1.call-done, bf16[384,3584]{1,0:T(8,128)(2,1)} %gather_fusion, pred[384]{0:T(512)(128)(4,1)S(1)} %get-tuple-element.2, pred[384]{0:T(512)(128)(4,1)S(1)} %get-tuple-element.6, pred[384,1024]{1,0:T(32,128)(4,1)S(1)} %copy.32, ...), kind=kOutput, calls=%fused_computation.8 | convolution fusion | flops 2828009472 | bytes 14813440 | tf_op jit(solution)/shard_map/dot_general | solution.py:47
  172.5 5.3 %reshape.123 = bf16[32,12,3584]{2,1,0:T(8,128)(2,1)} reshape(bf16[384,3584]{1,0:T(8,128)(2,1)} %fusion.1) | data formatting | bytes 5505024 | tf_op jit(solution)/shard_map/reshape | solution.py:78
  177.9 9.2 %all-to-all-start.2 = ((bf16[32,12,3584]{2,1,0:T(8,128)(2,1)}), bf16[32,12,3584]{2,1,0:T(8,128)(2,1)}, u32[]{:S(2)}, u32[]{:S(2)}) async-start(bf16[32,12,3584]{2,1,0:T(8,128)(2,1)} %reshape.123), calls=%async_computation.2 | async-start | bytes 7340032 | tf_op jit(solution)/shard_map/all_to_all | solution.py:77
  187.2 2.4 gather_fusion.2
  189.7 79.4 %all-to-all-done.2 = bf16[32,12,3584]{2,1,0:T(8,128)(2,1)} async-done(((bf16[32,12,3584]{2,1,0:T(8,128)(2,1)}), bf16[32,12,3584]{2,1,0:T(8,128)(2,1)}, u32[]{:S(2)}, u32[]{:S(2)}) %all-to-all-start.2) | async-done | bytes 2752544 | tf_op jit(solution)/shard_map/all_to_all | solution.py:77
  269.1 3.8 %reshape.124 = bf16[384,3584]{1,0:T(8,128)(2,1)S(1)} reshape(bf16[32,12,3584]{2,1,0:T(8,128)(2,1)} %all-to-all-done.2) | data formatting | bytes 5505024 | tf_op jit(solution)/shard_map/reshape | solution.py:84
  272.9 3.0 %gather_fusion.1 = bf16[256,3584]{1,0:T(8,128)(2,1)} fusion(bf16[384,3584]{1,0:T(8,128)(2,1)S(1)} %reshape.124, s32[1024]{0:T(1024)S(1)} %pad_clamp_fusion), kind=kCustom, calls=%fused_computation.1 | custom fusion | bytes 3671040 | tf_op jit(solution)/shard_map/gather | solution.py:84
  275.9 3.2 %multiply_convert_fusion = bf16[256,3584]{1,0:T(8,128)(2,1)} fusion(bf16[256,3584]{1,0:T(8,128)(2,1)} %gather_fusion.1, f32[256]{0:T(256)S(1)} %copy-done), kind=kLoop, calls=%fused_computation.9 | loop fusion | flops 2752512 | bytes 3671040 | tf_op jit(solution)/shard_map/convert_element_type | solution.py:86
  (30 shorter events, 1.2 us)
Async XLA Ops:
  7.2 128.2 %all-gather.2.cloned.1.call-start = ((), (), s32[]{:S(2)}) async-start(), calls=%async_computation.4 | async-start | bytes 7798784 | tf_op jit(solution)/shard_map/all_gather | solution.py:36
  14.0 23.4 %all-to-all-start = ((s32[32,12,9]{1,2,0:T(8,128)}), s32[32,12,9]{1,2,0:T(8,128)S(1)}, u32[]{:S(2)}, u32[]{:S(2)}) async-start(s32[32,12,9]{1,2,0:T(8,128)} %copy.28), calls=%async_computation | async-start | bytes 524288 | tf_op jit(solution)/shard_map/all_to_all | solution.py:72
  37.4 92.6 %all-to-all-start.1 = ((bf16[32,12,3584]{2,1,0:T(8,128)(2,1)}), bf16[32,12,3584]{2,1,0:T(8,128)(2,1)}, u32[]{:S(2)}, u32[]{:S(2)}) async-start(bf16[32,12,3584]{2,1,0:T(8,128)(2,1)} %reshape.121), calls=%async_computation.1 | async-start | bytes 7340032 | tf_op jit(solution)/shard_map/all_to_all | solution.py:69
  146.5 31.3 %all-to-all-start.3 = ((bf16[32,1,12]{2,1,0:T(2,128)(2,1)}), bf16[32,1,12]{2,1,0:T(2,128)(2,1)S(1)}, u32[]{:S(2)}, u32[]{:S(2)}) async-start(bf16[32,1,12]{2,1,0:T(2,128)(2,1)} %copy.33), calls=%async_computation.3 | async-start | bytes 32768 | tf_op jit(solution)/shard_map/all_to_all | solution.py:80
  177.9 91.2 %all-to-all-start.2 = ((bf16[32,12,3584]{2,1,0:T(8,128)(2,1)}), bf16[32,12,3584]{2,1,0:T(8,128)(2,1)}, u32[]{:S(2)}, u32[]{:S(2)}) async-start(bf16[32,12,3584]{2,1,0:T(8,128)(2,1)} %reshape.123), calls=%async_computation.2 | async-start | bytes 7340032 | tf_op jit(solution)/shard_map/all_to_all | solution.py:77
  272.9 3.0 %copy-start = (f32[256]{0:T(256)S(1)}, f32[256]{0:T(256)}, u32[]{:S(2)}) copy-start(f32[256]{0:T(256)} %param.11) | copy-start | bytes 3076
Sparse Core Ops, SparseCore 0:
  10.1 59.1 all-gather.1
where the time goes:
time: 290 us; the launch traced here: 286 us
  waiting for transfers between devices  167 us (58%)
  local copies, waits for them, and re-layouts  46.7 us (16%)
  starting transfers between devices  36.1 us (12%)
  matrix products  14.7 us (5%)
  between operations  14.2 us (5%)
  other arithmetic  7.42 us (3%)
    all_to_all x1, waiting for transfers between devices, body(): lax.all_to_all(out_rows, 'clu', split_axis=0, concat_axis=0, tiled=True)  84.4 us
    all_to_all x1, waiting for transfers between devices, body(): lax.all_to_all(cached.reshape(owners, capacity, width), 'clu', split_axis...  79.4 us
    all_to_all x1, starting transfers between devices, body(): lax.all_to_all(out_tags, 'clu', split_axis=0, concat_axis=0, tiled=True)  13.7 us
    gather x1, local copies, waits for them, and re-layouts, cluster_work(): jnp.take(piece, jnp.clip(positive, 0, span - 1), axis=0).astype(jnp.float32)  11.6 us
    all_to_all x1, starting transfers between devices, body(): lax.all_to_all(cached.reshape(owners, capacity, width), 'clu', split_axis...  9.17 us
    dot_general x1, matrix products, cluster_work(): product = jnp.dot(probs, piece, preferred_element_type=jnp.float32)  8.4 us
    all_to_all x1, starting transfers between devices, body(): lax.all_to_all(out_rows, 'clu', split_axis=0, concat_axis=0, tiled=True)  7.13 us
    dot_general x1, matrix products, cluster_work(): lax.dot_general(arrived, lax.all_gather(bank, 'bank', axis=0, tiled=True)...  6.34 us
  transfers between devices with their start and end apart: 5, of which 3 were waited for; matrix products, arithmetic and copies ran while one was open for 17% of the time, Pallas kernels for 0%

commit v1 on v0

v1 whole, which is shorter than its diff:
```python
import functools
import math

import jax
import jax.numpy as jnp
from jax import lax
from jax.experimental import pallas as pl
from jax.experimental.pallas import tpu as pltpu
from jax.sharding import PartitionSpec as P

MESH = pl.DeviceIdType.MESH
D = 3584
NX, NZ, NY = 4, 8, 8
NA, NB = 20, 12
PIECES = NA + NB
CAP = 12
ROWS = 16
PART = 896
MAIN = 3 * PART
WIDE = MAIN + 128
QDEV = 256
BROWS = 64
HALF = BROWS // 2
KEYS = 1024
KTILE = 256
BASE = (0, NA * ROWS)
COUNT = (NA * ROWS, NB * ROWS)
SCALE = 3.0 / math.sqrt(D)
BF = jnp.bfloat16
F32 = jnp.float32


def dot(a, b):
    return jnp.dot(a, b, preferred_element_type=F32)


def dot_t(a, b):
    return lax.dot_general(a, b, (((1,), (1,)), ((), ())), preferred_element_type=F32)


def iota(shape, dim):
    return lax.broadcasted_iota(jnp.int32, shape, dim)


def ones_where(cond):
    return jnp.where(cond, 1.0, 0.0).astype(BF)


def offsets(k, part):
    if part == 0:
        return k // 5, lax.rem(k % 5 + (NZ - 2), NZ)
    k = k - NA
    return k // 3, lax.rem(k % 3 + (NZ - 1), NZ)


def kernel(
    cid_ref,
    lists_ref,
    pos_ref,
    weight_ref,
    q_hbm,
    bank_hbm,
    grad_ref,
    loss_ref,
    q,
    keys,
    out,
    arrived,
    back,
    home,
    lastq,
    lg,
    wts,
    lastg,
    acc,
    local_sem,
    z_sem,
    go_send,
    go_recv,
    back_send,
    back_recv,
    ring_send,
    ring_recv,
    sib_send,
    sib_recv,
):
    clu, bank = lax.axis_index("clu"), lax.axis_index("bank")
    x, z = clu // NZ, clu % NZ
    y, core = bank // 2, bank % 2
    sibling = (clu, y * 2 + 1 - core)
    across = (x * NZ + lax.rem(z + 4, NZ), bank)

    def beside(d):
        return (clu, lax.rem(y + (1 if d == 0 else NY - 1), NY) * 2 + core)

    def at(dx, dz):
        return (lax.rem(x + dx, NX) * NZ + lax.rem(z + dz, NZ), bank)

    def remote(src, dst, send, recv, dev):
        return pltpu.make_async_remote_copy(
            src_ref=src, dst_ref=dst, send_sem=send, recv_sem=recv, device_id=dev, device_id_type=MESH
        )

    barrier = pltpu.get_barrier_semaphore()

    def greet(k, _):
        dx, dz = offsets(k, 0)

        @pl.when(k != 2)
        def _():
            pl.semaphore_signal(barrier, inc=1, device_id=at(dx, dz), device_id_type=MESH)

        return 0

    lax.fori_loop(0, NA, greet, 0)
    for dev in (sibling, across, beside(0), beside(1)):
        pl.semaphore_signal(barrier, inc=1, device_id=dev, device_id_type=MESH)

    own = pl.multiple_of((y * 2 + core) * BROWS, BROWS)
    get_q = pltpu.make_async_copy(q_hbm, q, local_sem.at[0])
    get_q.start()
    get_bank = pltpu.make_async_copy(bank_hbm, keys.at[0, pl.ds(own, BROWS)], local_sem.at[1])
    get_bank.start()

    eye = iota((QDEV, QDEV), 0) == iota((QDEV, QDEV), 1)

    def to_row(col):
        return jnp.sum(jnp.where(eye, col, 0.0), axis=0, keepdims=True)

    def to_col(row):
        return jnp.sum(jnp.where(eye, row, 0.0), axis=1, keepdims=True)

    cid = to_row(cid_ref[...].astype(F32)).astype(jnp.int32)
    dx = ((cid >> 3) - x + NX) & (NX - 1)
    dz = ((cid & 7) - z + NZ) & (NZ - 1)
    second = (dz >= 3) & (dz <= 5)
    piece = jnp.where(second, NA + dx * 3 + dz - 3, dx * 5 + ((dz + 2) & 7))
    named = iota((PIECES, QDEV), 0) == piece
    earlier = ones_where(iota((QDEV, QDEV), 0) < iota((QDEV, QDEV), 1))
    rank = jnp.sum(jnp.where(named, dot(ones_where(named), earlier), 0.0), axis=0, keepdims=True)
    rank = rank.astype(jnp.int32)
    slot = piece * ROWS + rank
    slot_last = piece * ROWS + CAP + (rank & 3)
    turn = rank >> 2
    slot_col = to_col(slot.astype(F32)).astype(jnp.int32)
    slot_last_col = to_col(slot_last.astype(F32)).astype(jnp.int32)
    turn_col = to_col(turn.astype(F32)).astype(jnp.int32)
    weight_col = to_col(weight_ref[...])
    pos_col = to_col(pos_ref[...].astype(F32)).astype(jnp.int32)
    lane = iota((QDEV, 128), 1)
    listed = lists_ref[:, 0:1] == lane
    for j in range(1, lists_ref.shape[1]):
        listed = listed | (lists_ref[:, j : j + 1] == lane)
    labels = jnp.where(listed & (lane < 16), 1.0, 0.0)
    labels = jnp.where(lane == 16, (pos_col >> 6).astype(F32), labels)
    labels = jnp.where(lane == 17, (pos_col & 63).astype(F32), labels).astype(BF)

    pl.semaphore_wait(barrier, NA - 1 + 4)

    z_copy = remote(bank_hbm, keys.at[1, pl.ds(own, BROWS)], z_sem.at[0], z_sem.at[1], across)
    z_copy.start()

    def rows_of(part, d, s, h):
        src = lax.rem(y + (NY - s if d == 0 else s), NY) * 2 + core
        return keys.at[part, pl.ds(pl.multiple_of(src * BROWS + h * HALF, HALF), HALF)]

    def ring(part, d, s, h):
        ref = rows_of(part, d, s - 1, h)
        src = bank_hbm.at[pl.ds(h * HALF, HALF)] if part == 0 and s == 1 else ref
        return remote(src, ref, ring_send.at[part, d, s - 1, h], ring_recv.at[part, d, s - 1, h], beside(d))

    def to_sibling(part, d, s, h):
        ref = rows_of(part, d, s, h)
        src = bank_hbm.at[pl.ds(h * HALF, HALF)] if part == 0 and s == 0 else ref
        return remote(src, ref, sib_send.at[part, d, s, h], sib_recv.at[part, d, s, h], sibling)

    def halves(s, d):
        return (0, 1) if s < 4 else (d,)

    def ring_begin(part):
        for h in (0, 1):
            for d in (0, 1):
                ring(part, d, 1, h).start()
        for h in (0, 1):
            to_sibling(part, 0, 0, h).start()

    def ring_step(part, s, h):
        for d in (0, 1):
            if h in halves(s, d):
                ring(part, d, s, h).wait_recv()
                if s < 4 and h in halves(s + 1, d):
                    ring(part, d, s + 1, h).start()
                to_sibling(part, d, s, h).start()

    def ring_end(part):
        for h in (0, 1):
            to_sibling(part, 0, 0, h).wait()
        for s in range(1, 5):
            for d in (0, 1):
                for h in halves(s, d):
                    ring(part, d, s, h).wait_send()
                    to_sibling(part, d, s, h).wait()

    ring_begin(0)

    def piece_rows(ref, k):
        return ref.at[pl.ds(pl.multiple_of(k * ROWS, ROWS), ROWS)]

    def go(k, part):
        dx, dz = offsets(k, part)
        return remote(piece_rows(out, k), piece_rows(arrived, k), go_send.at[k], go_recv.at[k], at(dx, dz))

    def come(k, part):
        dx, dz = offsets(k, part)
        dev = at(lax.rem(NX - dx, NX), lax.rem(NZ - dz, NZ))
        return remote(piece_rows(back, k), piece_rows(home, k), back_send.at[k], back_recv.at[k], dev)

    SELF = (2, NA + 1)
    stay_go = [
        pltpu.make_async_copy(piece_rows(out, SELF[p]), piece_rows(arrived, SELF[p]), local_sem.at[2 + p])
        for p in (0, 1)
    ]
    stay_come = [
        pltpu.make_async_copy(piece_rows(back, SELF[p]), piece_rows(home, SELF[p]), local_sem.at[4 + p])
        for p in (0, 1)
    ]

    def each(lo, hi, part, act):
        def step(k, _):
            @pl.when(k != SELF[part])
            def _():
                act(k)

            return 0

        lax.fori_loop(lo, hi, step, 0)

    get_q.wait()

    def pack(base, count):
        row = base + iota((count, QDEV), 0)
        main = ones_where(row == slot)
        out[base : base + count, MAIN:WIDE] = dot(main, labels).astype(BF)

        def step(t, _):
            cols = pl.ds(pl.multiple_of(t * PART, 128), PART)
            last = ones_where((row == slot_last) & (turn == t))
            out[base : base + count, cols] = (dot(main, q[:, cols]) + dot(last, q[:, MAIN:D])).astype(BF)
            return 0

        lax.fori_loop(0, 3, step, 0)

    for base, count in ((0, 160), (160, 160)):
        pack(base, count)
        each(base // ROWS, (base + count) // ROWS, 0, lambda k: go(k, 0).start())
    stay_go[0].start()
    pack(BASE[1], COUNT[1])
    each(NA, PIECES, 1, lambda k: go(k, 1).start())
    stay_go[1].start()

    def gather_last(part):
        base, count = BASE[part], COUNT[part]
        i, j = iota((count, count), 0), iota((count, count), 1)
        total = None
        for t in range(3):
            pick = ones_where((i >> 4 == j >> 4) & ((i & 15) == (j & 15) - CAP + 4 * t) & ((j & 15) >= CAP))
            term = dot(pick, arrived[base : base + count, t * PART : (t + 1) * PART])
            total = term if total is None else total + term
        lastq[base : base + count, :] = total.astype(BF)

    def logits(part):
        base, count = BASE[part], COUNT[part]

        def step(j, _):
            rows = pl.ds(pl.multiple_of(j * KTILE, KTILE), KTILE)
            total = dot_t(arrived[base : base + count, 0:MAIN], keys[part, rows, 0:MAIN])
            total = total + dot_t(lastq[base : base + count, :], keys[part, rows, MAIN:D])
            lg[base : base + count, rows] = total * SCALE
            return 0

        lax.fori_loop(0, KEYS // KTILE, step, 0)

    def softmax(part):
        base, count = BASE[part], COUNT[part]
        sub = 64
        kblock = iota((128, KEYS), 1) >> 6
        spread = ones_where(kblock == iota((128, KEYS), 0))

        def step(i, _):
            rows = pl.ds(pl.multiple_of(base + i * sub, sub), sub)
            tags = arrived[rows, MAIN:WIDE]
            l = lg[rows, :]
            high = tags[:, 16:17].astype(F32)
            pos = (high * 64.0 + tags[:, 17:18].astype(F32)).astype(jnp.int32)
            key = iota((sub, KEYS), 1)
            allowed = (dot(tags, spread) > 0.5) | (key >> 6 == high.astype(jnp.int32))
            hot = key == pos
            usable = jnp.where(allowed, l, -1e30)
            top = jnp.max(usable, axis=1, keepdims=True)
            e = jnp.exp(usable - top)
            total = jnp.sum(e, axis=1, keepdims=True)
            lse = top + jnp.log(total)
            loss = lse - jnp.sum(jnp.where(hot, l, 0.0), axis=1, keepdims=True)
            probs = (e * (1.0 / total)).astype(BF).astype(F32)
            wts[rows, :] = jnp.where(hot, probs - 1.0, probs).astype(BF)
            back[rows, MAIN:WIDE] = jnp.where(iota((sub, 128), 1) == 0, loss, 0.0).astype(BF)
            return 0

        lax.fori_loop(0, count // sub, step, 0)

    def pull(part):
        base, count = BASE[part], COUNT[part]
        lastg[0:count, :] = (dot(wts[base : base + count, :], keys[part, :, MAIN:D]) * SCALE).astype(BF)
        i, j = iota((count, count), 0), iota((count, count), 1)
        upper = iota((count, PART), 0) & 15

        def step(t, _):
            cols = pl.ds(pl.multiple_of(t * PART, 128), PART)
            main = dot(wts[base : base + count, :], keys[part, :, cols]) * SCALE
            put = ones_where((i >> 4 == j >> 4) & ((i & 15) >= CAP) & ((j & 15) == (i & 15) - CAP + 4 * t))
            low = dot(put, lastg[0:count, :])
            back[base : base + count, cols] = jnp.where(upper < CAP, main, low).astype(BF)
            return 0

        lax.fori_loop(0, 3, step, 0)

    def unpack(part):
        base, count = BASE[part], COUNT[part]
        col = base + iota((QDEV, count), 1)
        main = ones_where(slot_col == col)

        def step(t, _):
            cols = pl.ds(pl.multiple_of(t * PART, 128), PART)
            last = ones_where((slot_last_col == col) & (turn_col == t))
            block = home[base : base + count, cols]
            if part == 0:
                acc[:, cols] = dot(main, block)
            else:
                grad_ref[:, cols] = ((acc[:, cols] + dot(main, block)) * weight_col).astype(BF)
            tail = dot(last, block)
            acc[:, MAIN:D] = tail if part == 0 else acc[:, MAIN:D] + tail
            return 0

        if part == 0:
            col0 = iota((QDEV, count), 1)
            total = None
            for t in range(3):
                cols = slice(t * PART, (t + 1) * PART)
                last = ones_where((slot_last_col == col0) & (turn_col == t))
                acc[:, cols] = dot(main, home[base : base + count, cols])
                term = dot(last, home[base : base + count, cols])
                total = term if total is None else total + term
            acc[:, MAIN:D] = total
        else:
            lax.fori_loop(0, 3, step, 0)
            grad_ref[:, MAIN:D] = (acc[:, MAIN:D] * weight_col).astype(BF)
        return dot(main, home[base : base + count, MAIN:WIDE])

    for s, h in ((1, 0), (1, 1), (2, 0), (2, 1), (3, 0), (3, 1)):
        ring_step(0, s, h)
    z_copy.wait_recv()
    ring_begin(1)
    ring_step(0, 4, 0)
    ring_step(0, 4, 1)
    ring_end(0)
    get_bank.wait()

    ring_step(1, 1, 0)
    each(0, NA, 0, lambda k: go(k, 0).wait_recv())
    stay_go[0].wait()
    gather_last(0)
    logits(0)
    ring_step(1, 1, 1)
    softmax(0)
    ring_step(1, 2, 0)
    pull(0)
    each(0, NA, 0, lambda k: come(k, 0).start())
    stay_come[0].start()
    ring_step(1, 2, 1)
    each(NA, PIECES, 1, lambda k: go(k, 1).wait_recv())
    stay_go[1].wait()
    gather_last(1)
    for s, h in ((3, 0), (3, 1), (4, 0), (4, 1)):
        ring_step(1, s, h)
    ring_end(1)

    logits(1)
    softmax(1)
    pull(1)
    each(NA, PIECES, 1, lambda k: come(k, 1).start())
    stay_come[1].start()

    each(0, NA, 0, lambda k: come(k, 0).wait_recv())
    stay_come[0].wait()
    losses = unpack(0)
    z_copy.wait_send()
    each(0, NA, 0, lambda k: go(k, 0).wait_send())
    each(NA, PIECES, 1, lambda k: go(k, 1).wait_send())
    each(0, NA, 0, lambda k: come(k, 0).wait_send())
    each(NA, PIECES, 1, lambda k: come(k, 1).wait_recv())
    stay_come[1].wait()
    losses = losses + unpack(1)
    loss_ref[...] = to_row(losses[:, 0:1])
    each(NA, PIECES, 1, lambda k: come(k, 1).wait_send())


def body(queries, bank, cluster_ids, block_lists, positive_ids, loss_weights):
    vmem = pl.BlockSpec(memory_space=pltpu.VMEM)
    hbm = pl.BlockSpec(memory_space=pl.ANY)
    dma = pltpu.SemaphoreType.DMA
    slots = (PIECES * ROWS, WIDE)
    grad, loss = pl.pallas_call(
        kernel,
        out_shape=(
            jax.ShapeDtypeStruct((QDEV, D), BF),
            jax.ShapeDtypeStruct((1, QDEV), F32),
        ),
        in_specs=[vmem, vmem, vmem, vmem, hbm, hbm],
        out_specs=(vmem, vmem),
        scratch_shapes=[
            pltpu.VMEM((QDEV, D), BF),
            pltpu.VMEM((2, KEYS, D), BF),
            pltpu.VMEM(slots, BF),
            pltpu.VMEM(slots, BF),
            pltpu.VMEM(slots, BF),
            pltpu.VMEM(slots, BF),
            pltpu.VMEM((PIECES * ROWS, PART), BF),
            pltpu.VMEM((PIECES * ROWS, KEYS), F32),
            pltpu.VMEM((PIECES * ROWS, KEYS), BF),
            pltpu.VMEM((COUNT[0], PART), BF),
            pltpu.VMEM((QDEV, D), F32),
            dma((6,)),
            dma((2,)),
            dma((PIECES,)),
            dma((PIECES,)),
            dma((PIECES,)),
            dma((PIECES,)),
            dma((2, 2, 4, 2)),
            dma((2, 2, 4, 2)),
            dma((2, 2, 5, 2)),
            dma((2, 2, 5, 2)),
        ],
        compiler_params=pltpu.CompilerParams(
            collective_id=0, has_side_effects=True, vmem_limit_bytes=60 * 1024 * 1024
        ),
        cost_estimate=pl.CostEstimate(flops=10**10, bytes_accessed=10**7, transcendentals=10**6),
    )(
        cluster_ids,
        block_lists,
        positive_ids.reshape(1, QDEV),
        loss_weights.reshape(1, QDEV),
        queries,
        bank,
    )
    return grad, loss.reshape(QDEV).astype(BF)


def solution(mesh):
    rows = P(("clu", "bank"), None)
    flat = P(("clu", "bank"))
    return jax.shard_map(
        body,
        mesh=mesh,
        in_specs=(rows, rows, rows, rows, flat, flat),
        out_specs=(rows, flat),
        check_vma=False,
    )
```

time: 290 us -> 130 us (0.45); the launches traced: 286 us -> 130 us
  waiting for transfers between devices: 167 us -> 0 us
  Pallas kernels: 0 us -> 122 us
  local copies, waits for them, and re-layouts: 46.7 us -> 5.79 us
  starting transfers between devices: 36.1 us -> 0 us
  matrix products: 14.7 us -> 0 us
  between operations: 14.2 us -> 0.64 us
  other arithmetic: 7.42 us -> 1.2 us
    all_to_all x4 -> x0, waiting for transfers between devices: 166 us -> none  [the longest x1 84.4 us: body(): lax.all_to_all(out_rows, 'clu', split_axis=0, concat_axis=0, tiled=True)]
    pallas_call x0 -> x1, Pallas kernels: none -> 122 us  [body(): pl.pallas_call(kernel, out_shape=(jax.ShapeDtypeStruct((QDEV, D), BF), ja...]
    all_to_all x4 -> x0, starting transfers between devices: 36 us -> none  [the longest x1 13.7 us: body(): lax.all_to_all(out_tags, 'clu', split_axis=0, concat_axis=0, tiled=True)]
    gather x4 -> x0, local copies, waits for them, and re-layouts: 20.5 us -> none  [the longest x1 11.6 us: cluster_work(): jnp.take(piece, jnp.clip(positive, 0, span - 1), axis=0).astype(jnp.float32)]
    reshape x8 -> x0, local copies, waits for them, and re-layouts: 18.3 us -> none  [the longest x1 5.37 us: body(): lax.all_to_all(out_rows, 'clu', split_axis=0, concat_axis=0, tiled=True)]
    dot_general x2 -> x0, matrix products: 14.7 us -> none  [the longest x1 8.4 us: cluster_work(): product = jnp.dot(probs, piece, preferred_element_type=jnp.float32)]
    scatter x3 -> x0, local copies, waits for them, and re-layouts: 6.22 us -> none  [the longest x1 4.93 us: body(): jnp.zeros((total_slots, width), jnp.bfloat16).at[slot].set(queries)]
    unnamed x3, local copies, waits for them, and re-layouts: 0.01 us -> 5.79 us
  transfers between devices with their start and end apart: 5 -> 0, of which waited for: 3 -> 0; matrix products, arithmetic and copies ran while one was open for 17% -> 0% of each run, Pallas kernels for 0% -> 0%
where the time goes in v1:
time: 130 us
  Pallas kernels  122 us (94%)
  local copies, waits for them, and re-layouts  5.79 us (4%)
    pallas_call x1, Pallas kernels, body(): pl.pallas_call(kernel, out_shape=(jax.ShapeDtypeStruct((QDEV, D), BF), ja...  122 us
    unnamed x3, local copies, waits for them, and re-layouts  5.79 us

profile of v1, /device:TPU:1, one launch (start us, length us, event | category | flops | bytes accessed | tf_op | source)
XLA Modules:
  0.0 130.1 jit_solution(2390338831413881310)
XLA Ops:
  0.6 1.5 %copy.8.cid_ref = s32[256,1]{1,0:T(8,128)} copy(s32[256,1]{0,1:T(1,128)} %param.8) | data formatting | bytes 2048 | tf_op args[2]
  2.1 1.5 %copy.9.lists_ref = s32[256,8]{1,0:T(8,128)} copy(s32[256,8]{0,1:T(8,128)} %param.9) | data formatting | bytes 16384 | tf_op args[3]
  3.6 122.4 %shard_map.77 = (bf16[256,3584]{1,0:T(8,128)(2,1)}, f32[1,256]{1,0:T(1,128)}) custom-call(s32[256,1]{1,0:T(8,128)} %copy.8.cid_ref, s32[256,8]{1,0:T(8,128)} %copy.9.lists_ref, s32[1,256]{1,0:T(1,128)} %bitcast.2, f32[1,256]{1,0:T(1,128)} %bitcast.3, bf16[256,3584]{1,0:T(8,128)(2,1)} %q_hbm.1, bf16[64,3584]{1,0:T(8,128)(2,1)} %bank_hbm.1), custom_call_target="tpu_custom_call" | custom-call | flops 10000000000 | bytes 10000000 | tf_op jit(solution)/shard_map/pallas_call | solution.py:412
  126.0 1.2 convert_reduce_fusion
  127.2 2.8 %copy.11 = bf16[256,3584]{1,0:T(8,128)(2,1)} copy(bf16[256,3584]{1,0:T(8,128)(2,1)} %get-tuple-element.8) | data formatting | bytes 3670016

commit v2 on v1

v2 whole, which is shorter than its diff:
```python
import functools
import math

import jax
import jax.numpy as jnp
from jax import lax
from jax.experimental import pallas as pl
from jax.experimental.pallas import tpu as pltpu
from jax.sharding import PartitionSpec as P

MESH = pl.DeviceIdType.MESH
D = 3584
NX, NZ, NY = 4, 8, 8
NA, NB = 20, 12
PIECES = NA + NB
CAP = 12
ROWS = 16
PART = 896
MAIN = 3 * PART
WIDE = MAIN + 128
QDEV = 256
BROWS = 64
HALF = BROWS // 2
KEYS = 1024
KTILE = 256
BASE = (0, NA * ROWS)
COUNT = (NA * ROWS, NB * ROWS)
SCALE = 3.0 / math.sqrt(D)
BF = jnp.bfloat16
F32 = jnp.float32


def dot(a, b):
    return jnp.dot(a, b, preferred_element_type=F32)


def dot_t(a, b):
    return lax.dot_general(a, b, (((1,), (1,)), ((), ())), preferred_element_type=F32)


def iota(shape, dim):
    return lax.broadcasted_iota(jnp.int32, shape, dim)


def ones_where(cond):
    return jnp.where(cond, 1.0, 0.0).astype(BF)


def offsets(k, part):
    k = k - part * NA
    turn, dx = k // NX, k % NX
    odd = turn % 2
    return dx, odd * ((turn + 1) // 2) + (1 - odd) * lax.rem(NZ - turn // 2, NZ)


def kernel(
    cid_ref,
    lists_ref,
    pos_ref,
    q_hbm,
    bank_hbm,
    place_ref,
    home_hbm,
    q,
    keys,
    out,
    arrived,
    back,
    lastq,
    lg,
    wts,
    lastg,
    local_sem,
    z_sem,
    go_send,
    go_recv,
    back_send,
    back_recv,
    ring_send,
    ring_recv,
    sib_send,
    sib_recv,
):
    clu, bank = lax.axis_index("clu"), lax.axis_index("bank")
    x, z = clu // NZ, clu % NZ
    y, core = bank // 2, bank % 2
    sibling = (clu, y * 2 + 1 - core)
    across = (x * NZ + lax.rem(z + 4, NZ), bank)

    def beside(d):
        return (clu, lax.rem(y + (1 if d == 0 else NY - 1), NY) * 2 + core)

    def at(dx, dz):
        return (lax.rem(x + dx, NX) * NZ + lax.rem(z + dz, NZ), bank)

    def remote(src, dst, send, recv, dev):
        return pltpu.make_async_remote_copy(
            src_ref=src, dst_ref=dst, send_sem=send, recv_sem=recv, device_id=dev, device_id_type=MESH
        )

    barrier = pltpu.get_barrier_semaphore()

    def greet(k, _):
        dx, dz = offsets(k, 0)

        @pl.when(k != 0)
        def _():
            pl.semaphore_signal(barrier, inc=1, device_id=at(dx, dz), device_id_type=MESH)

        return 0

    lax.fori_loop(0, NA, greet, 0)
    for dev in (sibling, across, beside(0), beside(1)):
        pl.semaphore_signal(barrier, inc=1, device_id=dev, device_id_type=MESH)

    own = pl.multiple_of((y * 2 + core) * BROWS, BROWS)
    get_q = pltpu.make_async_copy(q_hbm, q, local_sem.at[0])
    get_q.start()
    get_bank = pltpu.make_async_copy(bank_hbm, keys.at[0, pl.ds(own, BROWS)], local_sem.at[1])
    get_bank.start()

    pl.semaphore_wait(barrier, NA - 1 + 4)

    def z_copy(h):
        to = keys.at[1, pl.ds(pl.multiple_of(own + h * HALF, HALF), HALF)]
        return remote(bank_hbm.at[pl.ds(h * HALF, HALF)], to, z_sem.at[0, h], z_sem.at[1, h], across)

    z_copy(0).start()
    z_copy(1).start()

    def rows_of(part, d, s, h):
        src = lax.rem(y + (NY - s if d == 0 else s), NY) * 2 + core
        return keys.at[part, pl.ds(pl.multiple_of(src * BROWS + h * HALF, HALF), HALF)]

    def ring(part, d, s, h):
        ref = rows_of(part, d, s - 1, h)
        src = bank_hbm.at[pl.ds(h * HALF, HALF)] if part == 0 and s == 1 else ref
        return remote(src, ref, ring_send.at[part, d, s - 1, h], ring_recv.at[part, d, s - 1, h], beside(d))

    def to_sibling(part, d, s, h):
        ref = rows_of(part, d, s, h)
        src = bank_hbm.at[pl.ds(h * HALF, HALF)] if part == 0 and s == 0 else ref
        return remote(src, ref, sib_send.at[part, d, s, h], sib_recv.at[part, d, s, h], sibling)

    def halves(s, d):
        return (0, 1) if s < 4 else (d,)

    def ring_begin(part):
        for h in (0, 1):
            if part == 1:
                z_copy(h).wait_recv()
            for d in (0, 1):
                ring(part, d, 1, h).start()
            to_sibling(part, 0, 0, h).start()

    def ring_step(part, s, h):
        for d in (0, 1):
            if h in halves(s, d):
                ring(part, d, s, h).wait_recv()
                if s < 4 and h in halves(s + 1, d):
                    ring(part, d, s + 1, h).start()
                to_sibling(part, d, s, h).start()

    def sibling_done(part, s):
        if s == 0:
            for h in (0, 1):
                to_sibling(part, 0, 0, h).wait_recv()
            return
        for d in (0, 1):
            for h in halves(s, d):
                to_sibling(part, d, s, h).wait_recv()

    def ring_end(part):
        for h in (0, 1):
            to_sibling(part, 0, 0, h).wait_send()
        for s in range(1, 5):
            for d in (0, 1):
                for h in halves(s, d):
                    ring(part, d, s, h).wait_send()
                    to_sibling(part, d, s, h).wait_send()

    ring_begin(0)

    cid = cid_ref[...]
    dx = ((cid >> 3) - x + NX) & (NX - 1)
    dz = ((cid & 7) - z + NZ) & (NZ - 1)
    second = (dz >= 3) & (dz <= 5)
    away = jnp.where(second, dz - 4, jnp.where(dz > 4, dz - NZ, dz))
    turn = jnp.where(away > 0, 2 * away - 1, -2 * away)
    piece = jnp.where(second, NA, 0) + turn * NX + dx
    named = iota((PIECES, QDEV), 0) == piece
    earlier = ones_where(iota((QDEV, QDEV), 0) < iota((QDEV, QDEV), 1))
    rank = jnp.sum(jnp.where(named, dot(ones_where(named), earlier), 0.0), axis=0, keepdims=True)
    rank = rank.astype(jnp.int32)
    slot = piece * ROWS + rank
    slot_last = piece * ROWS + CAP + (rank & 3)
    third = rank >> 2
    place_ref[0:1, :] = slot
    place_ref[1:2, :] = slot_last
    place_ref[2:3, :] = third
    lane = iota((128, QDEV), 0)
    listed = lists_ref[0:1, :] == lane
    for j in range(1, lists_ref.shape[0]):
        listed = listed | (lists_ref[j : j + 1, :] == lane)
    pos = pos_ref[...]
    labels = jnp.where(listed & (lane < 16), 1.0, 0.0)
    labels = jnp.where(lane == 16, (pos >> 6).astype(F32), labels)
    labels = jnp.where(lane == 17, (pos & 63).astype(F32), labels).astype(BF)

    def piece_rows(ref, k):
        return ref.at[pl.ds(pl.multiple_of(k * ROWS, ROWS), ROWS)]

    def go(k, part):
        dx, dz = offsets(k, part)
        return remote(piece_rows(out, k), piece_rows(arrived, k), go_send.at[k], go_recv.at[k], at(dx, dz))

    GROUPS = ((0, PART), (PART, PART), (2 * PART, PART + 128))

    def come(k, part, t):
        dx, dz = offsets(k, part)
        dev = at(lax.rem(NX - dx, NX), lax.rem(NZ - dz, NZ))
        cols = pl.ds(*GROUPS[t])
        src, to = piece_rows(back, k).at[:, cols], piece_rows(home_hbm, k).at[:, cols]
        return remote(src, to, back_send.at[t, k], back_recv.at[t, k], dev)

    SELF = (0, NA)
    stay_go = [
        pltpu.make_async_copy(piece_rows(out, SELF[p]), piece_rows(arrived, SELF[p]), local_sem.at[2 + p])
        for p in (0, 1)
    ]
    stay_come = [
        pltpu.make_async_copy(piece_rows(back, SELF[p]), piece_rows(home_hbm, SELF[p]), local_sem.at[4 + p])
        for p in (0, 1)
    ]

    def each(lo, hi, part, act):
        def step(k, _):
            @pl.when(k != SELF[part])
            def _():
                act(k)

            return 0

        lax.fori_loop(lo, hi, step, 0)

    get_q.wait()

    def pack(base, count):
        row = base + iota((count, QDEV), 0)
        main = ones_where(row == slot)
        out[base : base + count, MAIN:WIDE] = dot_t(main, labels).astype(BF)

        def step(t, _):
            cols = pl.ds(pl.multiple_of(t * PART, 128), PART)
            last = ones_where((row == slot_last) & (third == t))
            out[base : base + count, cols] = (dot(main, q[:, cols]) + dot(last, q[:, MAIN:D])).astype(BF)
            return 0

        lax.fori_loop(0, 3, step, 0)

    for base, count in ((0, 160), (160, 160)):
        pack(base, count)
        each(base // ROWS, (base + count) // ROWS, 0, lambda k: go(k, 0).start())
    stay_go[0].start()
    pack(BASE[1], COUNT[1])

    def gather_last(part):
        base, count = BASE[part], COUNT[part]
        i, j = iota((count, count), 0), iota((count, count), 1)
        total = None
        for t in range(3):
            pick = ones_where((i >> 4 == j >> 4) & ((i & 15) == (j & 15) - CAP + 4 * t) & ((j & 15) >= CAP))
            term = dot(pick, arrived[base : base + count, t * PART : (t + 1) * PART])
            total = term if total is None else total + term
        lastq[base : base + count, :] = total.astype(BF)

    def logits(part, begin, steps, size):
        base, count = BASE[part], COUNT[part]

        def step(j, _):
            rows = pl.ds(pl.multiple_of(lax.rem((begin + j) * size, KEYS), size), size)
            total = dot_t(arrived[base : base + count, 0:MAIN], keys[part, rows, 0:MAIN])
            total = total + dot_t(lastq[base : base + count, :], keys[part, rows, MAIN:D])
            lg[base : base + count, rows] = total * SCALE
            return 0

        lax.fori_loop(0, steps, step, 0)

    def softmax(part):
        base, count = BASE[part], COUNT[part]
        sub = 64
        kblock = iota((128, KEYS), 1) >> 6
        spread = ones_where(kblock == iota((128, KEYS), 0))

        def step(i, _):
            rows = pl.ds(pl.multiple_of(base + i * sub, sub), sub)
            tags = arrived[rows, MAIN:WIDE]
            l = lg[rows, :]
            high = tags[:, 16:17].astype(F32)
            pos = (high * 64.0 + tags[:, 17:18].astype(F32)).astype(jnp.int32)
            key = iota((sub, KEYS), 1)
            allowed = (dot(tags, spread) > 0.5) | (key >> 6 == high.astype(jnp.int32))
            hot = key == pos
            usable = jnp.where(allowed, l, -1e30)
            top = jnp.max(usable, axis=1, keepdims=True)
            e = jnp.exp(usable - top)
            total = jnp.sum(e, axis=1, keepdims=True)
            lse = top + jnp.log(total)
            loss = lse - jnp.sum(jnp.where(hot, l, 0.0), axis=1, keepdims=True)
            probs = (e * (1.0 / total)).astype(BF).astype(F32)
            wts[rows, :] = jnp.where(hot, probs - 1.0, probs).astype(BF)
            back[rows, MAIN:WIDE] = jnp.where(iota((sub, 128), 1) == 0, loss, 0.0).astype(BF)
            return 0

        lax.fori_loop(0, count // sub, step, 0)

    def pull(part, sent):
        base, count = BASE[part], COUNT[part]
        lastg[0:count, :] = (dot(wts[base : base + count, :], keys[part, :, MAIN:D]) * SCALE).astype(BF)
        i, j = iota((count, count), 0), iota((count, count), 1)
        upper = iota((count, 1), 0) & 15

        for t in range(3):
            cols = slice(t * PART, (t + 1) * PART)
            main = dot(wts[base : base + count, :], keys[part, :, cols]) * SCALE
            put = ones_where((i >> 4 == j >> 4) & ((i & 15) >= CAP) & ((j & 15) == (i & 15) - CAP + 4 * t))
            low = dot(put, lastg[0:count, :])
            back[base : base + count, cols] = jnp.where(upper < CAP, main, low).astype(BF)
            sent(t)

    for s, h in ((1, 0), (1, 1), (2, 0), (2, 1), (3, 0), (3, 1)):
        ring_step(0, s, h)
    ring_begin(1)
    ring_step(0, 4, 0)
    ring_step(0, 4, 1)
    for i in range(5):
        sibling_done(0, i)
    get_bank.wait()

    each(0, NA, 0, lambda k: go(k, 0).wait_recv())
    stay_go[0].wait()
    each(NA, PIECES, 1, lambda k: go(k, 1).start())
    stay_go[1].start()
    gather_last(0)
    ring_step(1, 1, 0)
    logits(0, 0, KEYS // KTILE, KTILE)
    ring_step(1, 1, 1)
    softmax(0)
    ring_step(1, 2, 0)

    def sent_first(t):
        each(0, NA, 0, lambda k: come(k, 0, t).start())
        if t == 2:
            stay_come[0].start()

    pull(0, sent_first)
    ring_step(1, 2, 1)
    each(NA, PIECES, 1, lambda k: go(k, 1).wait_recv())
    stay_go[1].wait()
    gather_last(1)
    ring_step(1, 3, 0)
    ring_step(1, 3, 1)
    for i in range(3):
        sibling_done(1, i)
    logits(1, y + NY - 2, 5, 2 * BROWS)
    sibling_done(1, 3)
    logits(1, y + 3, 1, 2 * BROWS)
    logits(1, y + 5, 1, 2 * BROWS)
    ring_step(1, 4, 0)
    ring_step(1, 4, 1)
    sibling_done(1, 4)

    logits(1, y + 4, 1, 2 * BROWS)
    softmax(1)

    def sent_second(t):
        each(NA, PIECES, 1, lambda k: come(k, 1, t).start())
        if t == 2:
            stay_come[1].start()

    pull(1, sent_second)
    ring_end(0)
    ring_end(1)
    z_copy(0).wait_send()
    z_copy(1).wait_send()
    each(0, NA, 0, lambda k: go(k, 0).wait_send())
    each(NA, PIECES, 1, lambda k: go(k, 1).wait_send())

    stay_come[0].wait()
    stay_come[1].wait()
    for t in range(3):
        each(0, NA, 0, lambda k: come(k, 0, t).wait_send())
        each(0, NA, 0, lambda k: come(k, 0, t).wait_recv())
    for t in range(3):
        each(NA, PIECES, 1, lambda k: come(k, 1, t).wait_send())
        each(NA, PIECES, 1, lambda k: come(k, 1, t).wait_recv())


def finish(place_ref, weight_ref, home_hbm, grad_hbm, loss_ref, home, grad, in_sem, out_sem):
    def get(t):
        cols = pl.ds(t * PART, PART) if t < 3 else pl.ds(MAIN, 128)
        return pltpu.make_async_copy(home_hbm.at[:, cols], home.at[:, cols], in_sem.at[t])

    def put(t):
        cols = pl.ds(t * PART, PART)
        return pltpu.make_async_copy(grad.at[:, cols], grad_hbm.at[:, cols], out_sem.at[t])

    for t in range(4):
        get(t).start()
    eye = iota((QDEV, QDEV), 0) == iota((QDEV, QDEV), 1)

    def to_row(col):
        return jnp.sum(jnp.where(eye, col, 0.0), axis=0, keepdims=True)

    def to_col(row):
        return jnp.sum(jnp.where(eye, row, 0.0), axis=1, keepdims=True)

    slot, slot_last, third = [to_col(place_ref[i : i + 1, :].astype(F32)).astype(jnp.int32) for i in range(3)]
    weight = to_col(weight_ref[...])
    col = iota((QDEV, PIECES * ROWS), 1)
    main = ones_where(slot == col)
    total = None
    for t in range(3):
        cols = slice(t * PART, (t + 1) * PART)
        get(t).wait()
        grad[:, cols] = (dot(main, home[:, cols]) * weight).astype(BF)
        put(t).start()
        term = dot(ones_where((slot_last == col) & (third == t)), home[:, cols])
        total = term if total is None else total + term
    grad[:, MAIN:D] = (total * weight).astype(BF)
    put(3).start()
    get(3).wait()
    losses = dot(main, home[:, MAIN:WIDE])
    loss_ref[...] = to_row(losses[:, 0:1]).reshape(QDEV).astype(BF)
    for t in range(4):
        put(t).wait()


def body(queries, bank, cluster_ids, block_lists, positive_ids, loss_weights):
    vmem = pl.BlockSpec(memory_space=pltpu.VMEM)
    hbm = pl.BlockSpec(memory_space=pl.ANY)
    dma = pltpu.SemaphoreType.DMA
    slots = (PIECES * ROWS, WIDE)
    place, home = pl.pallas_call(
        kernel,
        out_shape=(
            jax.ShapeDtypeStruct((8, QDEV), jnp.int32),
            jax.ShapeDtypeStruct(slots, BF),
        ),
        in_specs=[vmem, vmem, vmem, hbm, hbm],
        out_specs=(vmem, hbm),
        scratch_shapes=[
            pltpu.VMEM((QDEV, D), BF),
            pltpu.VMEM((2, KEYS, D), BF),
            pltpu.VMEM(slots, BF),
            pltpu.VMEM(slots, BF),
            pltpu.VMEM(slots, BF),
            pltpu.VMEM((PIECES * ROWS, PART), BF),
            pltpu.VMEM((PIECES * ROWS, KEYS), F32),
            pltpu.VMEM((PIECES * ROWS, KEYS), BF),
            pltpu.VMEM((COUNT[0], PART), BF),
            dma((6,)),
            dma((2, 2)),
            dma((PIECES,)),
            dma((PIECES,)),
            dma((3, PIECES)),
            dma((3, PIECES)),
            dma((2, 2, 4, 2)),
            dma((2, 2, 4, 2)),
            dma((2, 2, 5, 2)),
            dma((2, 2, 5, 2)),
        ],
        compiler_params=pltpu.CompilerParams(
            collective_id=0, has_side_effects=True, vmem_limit_bytes=60 * 1024 * 1024
        ),
        cost_estimate=pl.CostEstimate(flops=10**10, bytes_accessed=10**7, transcendentals=10**6),
    )(cluster_ids.reshape(1, QDEV), block_lists.T, positive_ids.reshape(1, QDEV), queries, bank)
    grad, loss = pl.pallas_call(
        finish,
        out_shape=(jax.ShapeDtypeStruct((QDEV, D), BF), jax.ShapeDtypeStruct((QDEV,), BF)),
        in_specs=[vmem, vmem, hbm],
        out_specs=(hbm, vmem),
        scratch_shapes=[
            pltpu.VMEM(slots, BF),
            pltpu.VMEM((QDEV, D), BF),
            dma((4,)),
            dma((4,)),
        ],
        compiler_params=pltpu.CompilerParams(vmem_limit_bytes=60 * 1024 * 1024),
        cost_estimate=pl.CostEstimate(flops=10**9, bytes_accessed=5 * 10**6, transcendentals=0),
    )(place, loss_weights.reshape(1, QDEV), home)
    return grad, loss


def solution(mesh):
    rows = P(("clu", "bank"), None)
    flat = P(("clu", "bank"))
    return jax.shard_map(
        body,
        mesh=mesh,
        in_specs=(rows, rows, rows, rows, flat, flat),
        out_specs=(rows, flat),
        check_vma=False,
    )
```

time: 130 us -> 126 us (0.969)
  local copies, waits for them, and re-layouts: 5.79 us -> 0 us
  Pallas kernels: 122 us -> 125 us
    unnamed x3 -> x0, local copies, waits for them, and re-layouts: 5.79 us -> none
    pallas_call x1 -> x2, Pallas kernels: 122 us -> 125 us  [the longest x1 119 us: body(): pl.pallas_call(kernel, out_shape=(jax.ShapeDtypeStruct((8, QDEV), jnp.int...]
where the time goes in v2:
time: 126 us; the launch traced here: 125 us
  Pallas kernels  125 us (99%)
    pallas_call x1, Pallas kernels, body(): pl.pallas_call(kernel, out_shape=(jax.ShapeDtypeStruct((8, QDEV), jnp.int...  119 us
    pallas_call x1, Pallas kernels, body(): pl.pallas_call(finish, out_shape=(jax.ShapeDtypeStruct((QDEV, D), BF), ja...  5.44 us

profile of v2, /device:TPU:1, one launch (start us, length us, event | category | flops | bytes accessed | tf_op | source)
XLA Modules:
  0.0 125.4 jit_solution(18101755229673009990)
XLA Ops:
  0.6 119.2 %shard_map.77 = (s32[8,256]{1,0:T(8,128)}, bf16[512,2816]{1,0:T(8,128)(2,1)}) custom-call(s32[1,256]{1,0:T(1,128)} %bitcast.5, s32[8,256]{1,0:T(8,128)} %bitcast.4, s32[1,256]{1,0:T(1,128)} %bitcast.6, bf16[256,3584]{1,0:T(8,128)(2,1)} %q_hbm.1, bf16[64,3584]{1,0:T(8,128)(2,1)} %bank_hbm.1), custom_call_target="tpu_custom_call" | custom-call | flops 10000000000 | bytes 10000000 | tf_op jit(solution)/shard_map/pallas_call | solution.py:444
  119.8 5.4 %shard_map.78 = (bf16[256,3584]{1,0:T(8,128)(2,1)}, bf16[256]{0:T(256)(128)(2,1)}) custom-call(s32[8,256]{1,0:T(8,128)} %get-tuple-element.4.place_ref, f32[1,256]{1,0:T(1,128)} %bitcast.7, bf16[512,2816]{1,0:T(8,128)(2,1)} %get-tuple-element.5.home_hbm), custom_call_target="tpu_custom_call" | custom-call | flops 1000000000 | bytes 5000000 | tf_op jit(solution)/shard_map/pallas_call | solution.py:478

commit v3 on v2

--- a/solution.py
+++ b/solution.py
@@ -57,6 +57,7 @@
     cid_ref,
     lists_ref,
     pos_ref,
+    weight_ref,
     q_hbm,
     bank_hbm,
     place_ref,
@@ -195,9 +196,6 @@
     slot = piece * ROWS + rank
     slot_last = piece * ROWS + CAP + (rank & 3)
     third = rank >> 2
-    place_ref[0:1, :] = slot
-    place_ref[1:2, :] = slot_last
-    place_ref[2:3, :] = third
     lane = iota((128, QDEV), 0)
     listed = lists_ref[0:1, :] == lane
     for j in range(1, lists_ref.shape[0]):
@@ -212,7 +210,7 @@
 
     def go(k, part):
         dx, dz = offsets(k, part)
-        return remote(piece_rows(out, k), piece_rows(arrived, k), go_send.at[k], go_recv.at[k], at(dx, dz))
+        return remote(piece_rows(out, k), piece_rows(arrived, k), go_send.at[part], go_recv.at[part], at(dx, dz))
 
     GROUPS = ((0, PART), (PART, PART), (2 * PART, PART + 128))
 
@@ -221,7 +219,16 @@
         dev = at(lax.rem(NX - dx, NX), lax.rem(NZ - dz, NZ))
         cols = pl.ds(*GROUPS[t])
         src, to = piece_rows(back, k).at[:, cols], piece_rows(home_hbm, k).at[:, cols]
-        return remote(src, to, back_send.at[t, k], back_recv.at[t, k], dev)
+        return remote(src, to, back_send.at[part], back_recv.at[part], dev)
+
+    def others(ref, part):
+        return ref.at[pl.ds(BASE[part] + ROWS, COUNT[part] - ROWS)]
+
+    def all_go(part):
+        return remote(others(out, part), others(arrived, part), go_send.at[part], go_recv.at[part], sibling)
+
+    def all_come(part):
+        return remote(others(back, part), others(home_hbm, part), back_send.at[part], back_recv.at[part], sibling)
 
     SELF = (0, NA)
     stay_go = [
@@ -337,7 +344,7 @@
         sibling_done(0, i)
     get_bank.wait()
 
-    each(0, NA, 0, lambda k: go(k, 0).wait_recv())
+    all_go(0).wait_recv()
     stay_go[0].wait()
     each(NA, PIECES, 1, lambda k: go(k, 1).start())
     stay_go[1].start()
@@ -355,17 +362,23 @@
 
     pull(0, sent_first)
     ring_step(1, 2, 1)
-    each(NA, PIECES, 1, lambda k: go(k, 1).wait_recv())
+    all_go(1).wait_recv()
     stay_go[1].wait()
     gather_last(1)
     ring_step(1, 3, 0)
     ring_step(1, 3, 1)
+    eye = iota((QDEV, QDEV), 0) == iota((QDEV, QDEV), 1)
+    lane = iota((QDEV, 128), 1)
+    for i, row in enumerate((slot.astype(F32), slot_last.astype(F32), third.astype(F32), weight_ref[...])):
+        column = jnp.sum(jnp.where(eye, row, 0.0), axis=1, keepdims=True)
+        place_ref[...] = jnp.where(lane == i, column, 0.0 if i == 0 else place_ref[...])
     for i in range(3):
         sibling_done(1, i)
     logits(1, y + NY - 2, 5, 2 * BROWS)
     sibling_done(1, 3)
     logits(1, y + 3, 1, 2 * BROWS)
     logits(1, y + 5, 1, 2 * BROWS)
+    ring_end(0)
     ring_step(1, 4, 0)
     ring_step(1, 4, 1)
     sibling_done(1, 4)
@@ -379,24 +392,20 @@
             stay_come[1].start()
 
     pull(1, sent_second)
-    ring_end(0)
     ring_end(1)
     z_copy(0).wait_send()
     z_copy(1).wait_send()
-    each(0, NA, 0, lambda k: go(k, 0).wait_send())
-    each(NA, PIECES, 1, lambda k: go(k, 1).wait_send())
+    all_go(0).wait_send()
+    all_go(1).wait_send()
 
     stay_come[0].wait()
     stay_come[1].wait()
-    for t in range(3):
-        each(0, NA, 0, lambda k: come(k, 0, t).wait_send())
-        each(0, NA, 0, lambda k: come(k, 0, t).wait_recv())
-    for t in range(3):
-        each(NA, PIECES, 1, lambda k: come(k, 1, t).wait_send())
-        each(NA, PIECES, 1, lambda k: come(k, 1, t).wait_recv())
-
-
-def finish(place_ref, weight_ref, home_hbm, grad_hbm, loss_ref, home, grad, in_sem, out_sem):
+    for part in (0, 1):
+        all_come(part).wait_send()
+        all_come(part).wait_recv()
+
+
+def finish(place_ref, home_hbm, grad_hbm, loss_ref, home, grad, in_sem, out_sem):
     def get(t):
         cols = pl.ds(t * PART, PART) if t < 3 else pl.ds(MAIN, 128)
         return pltpu.make_async_copy(home_hbm.at[:, cols], home.at[:, cols], in_sem.at[t])
@@ -407,31 +416,26 @@
 
     for t in range(4):
         get(t).start()
-    eye = iota((QDEV, QDEV), 0) == iota((QDEV, QDEV), 1)
-
-    def to_row(col):
-        return jnp.sum(jnp.where(eye, col, 0.0), axis=0, keepdims=True)
-
-    def to_col(row):
-        return jnp.sum(jnp.where(eye, row, 0.0), axis=1, keepdims=True)
-
-    slot, slot_last, third = [to_col(place_ref[i : i + 1, :].astype(F32)).astype(jnp.int32) for i in range(3)]
-    weight = to_col(weight_ref[...])
+    slot, slot_last, third = [place_ref[:, i : i + 1].astype(jnp.int32) for i in range(3)]
+    weight = place_ref[:, 3:4]
     col = iota((QDEV, PIECES * ROWS), 1)
     main = ones_where(slot == col)
     total = None
     for t in range(3):
         cols = slice(t * PART, (t + 1) * PART)
         get(t).wait()
-        grad[:, cols] = (dot(main, home[:, cols]) * weight).astype(BF)
+        both = jnp.concatenate([main, ones_where((slot_last == col) & (third == t))], axis=0)
+        moved = dot(both, home[:, cols])
+        grad[:, cols] = (moved[:QDEV] * weight).astype(BF)
         put(t).start()
-        term = dot(ones_where((slot_last == col) & (third == t)), home[:, cols])
+        term = moved[QDEV:]
         total = term if total is None else total + term
     grad[:, MAIN:D] = (total * weight).astype(BF)
     put(3).start()
     get(3).wait()
     losses = dot(main, home[:, MAIN:WIDE])
-    loss_ref[...] = to_row(losses[:, 0:1]).reshape(QDEV).astype(BF)
+    eye = iota((QDEV, QDEV), 0) == iota((QDEV, QDEV), 1)
+    loss_ref[...] = jnp.sum(jnp.where(eye, losses[:, 0:1], 0.0), axis=0, keepdims=True).reshape(QDEV).astype(BF)
     for t in range(4):
         put(t).wait()
 
@@ -444,10 +448,10 @@
     place, home = pl.pallas_call(
         kernel,
         out_shape=(
-            jax.ShapeDtypeStruct((8, QDEV), jnp.int32),
+            jax.ShapeDtypeStruct((QDEV, 128), F32),
             jax.ShapeDtypeStruct(slots, BF),
         ),
-        in_specs=[vmem, vmem, vmem, hbm, hbm],
+        in_specs=[vmem, vmem, vmem, vmem, hbm, hbm],
         out_specs=(vmem, hbm),
         scratch_shapes=[
             pltpu.VMEM((QDEV, D), BF),
@@ -461,10 +465,10 @@
             pltpu.VMEM((COUNT[0], PART), BF),
             dma((6,)),
             dma((2, 2)),
-            dma((PIECES,)),
-            dma((PIECES,)),
-            dma((3, PIECES)),
-            dma((3, PIECES)),
+            dma((2,)),
+            dma((2,)),
+            dma((2,)),
+            dma((2,)),
             dma((2, 2, 4, 2)),
             dma((2, 2, 4, 2)),
             dma((2, 2, 5, 2)),
@@ -474,11 +478,18 @@
             collective_id=0, has_side_effects=True, vmem_limit_bytes=60 * 1024 * 1024
         ),
         cost_estimate=pl.CostEstimate(flops=10**10, bytes_accessed=10**7, transcendentals=10**6),
-    )(cluster_ids.reshape(1, QDEV), block_lists.T, positive_ids.reshape(1, QDEV), queries, bank)
+    )(
+        cluster_ids.reshape(1, QDEV),
+        block_lists.T,
+        positive_ids.reshape(1, QDEV),
+        loss_weights.reshape(1, QDEV),
+        queries,
+        bank,
+    )
     grad, loss = pl.pallas_call(
         finish,
         out_shape=(jax.ShapeDtypeStruct((QDEV, D), BF), jax.ShapeDtypeStruct((QDEV,), BF)),
-        in_specs=[vmem, vmem, hbm],
+        in_specs=[vmem, hbm],
         out_specs=(hbm, vmem),
         scratch_shapes=[
             pltpu.VMEM(slots, BF),
@@ -488,7 +499,7 @@
         ],
         compiler_params=pltpu.CompilerParams(vmem_limit_bytes=60 * 1024 * 1024),
         cost_estimate=pl.CostEstimate(flops=10**9, bytes_accessed=5 * 10**6, transcendentals=0),
-    )(place, loss_weights.reshape(1, QDEV), home)
+    )(place, home)
     return grad, loss
 
 

time: 126 us -> 123 us (0.976)
  Pallas kernels: 125 us -> 122 us
    pallas_call x1, Pallas kernels: 119 us -> 116 us  [body(): pl.pallas_call(kernel, out_shape=(jax.ShapeDtypeStruct((QDEV, 128), F32),...]
where the time goes in v3:
time: 123 us; the launch traced here: 122 us
  Pallas kernels  122 us (99%)
    pallas_call x1, Pallas kernels, body(): pl.pallas_call(kernel, out_shape=(jax.ShapeDtypeStruct((QDEV, 128), F32),...  116 us
    pallas_call x1, Pallas kernels, body(): pl.pallas_call(finish, out_shape=(jax.ShapeDtypeStruct((QDEV, D), BF), ja...  5.53 us

profile of v3, /device:TPU:1, one launch (start us, length us, event | category | flops | bytes accessed | tf_op | source)
XLA Modules:
  0.0 122.4 jit_solution(8984212142588794307)
XLA Ops:
  0.6 116.2 %shard_map.77 = (f32[256,128]{1,0:T(8,128)}, bf16[512,2816]{1,0:T(8,128)(2,1)}) custom-call(s32[1,256]{1,0:T(1,128)} %bitcast.5, s32[8,256]{1,0:T(8,128)} %bitcast.4, s32[1,256]{1,0:T(1,128)} %bitcast.6, f32[1,256]{1,0:T(1,128)} %bitcast.7, bf16[256,3584]{1,0:T(8,128)(2,1)} %q_hbm.1, bf16[64,3584]{1,0:T(8,128)(2,1)} %bank_hbm.1), custom_call_target="tpu_custom_call" | custom-call | flops 10000000000 | bytes 10000000 | tf_op jit(solution)/shard_map/pallas_call | solution.py:448
  116.9 5.5 %shard_map.78 = (bf16[256,3584]{1,0:T(8,128)(2,1)}, bf16[256]{0:T(256)(128)(2,1)}) custom-call(f32[256,128]{1,0:T(8,128)} %get-tuple-element.4.place_ref, bf16[512,2816]{1,0:T(8,128)(2,1)} %get-tuple-element.5.home_hbm), custom_call_target="tpu_custom_call" | custom-call | flops 1000000000 | bytes 5000000 | tf_op jit(solution)/shard_map/pallas_call | solution.py:489

commit v4 on v3

--- a/solution.py
+++ b/solution.py
@@ -60,7 +60,7 @@
     weight_ref,
     q_hbm,
     bank_hbm,
-    place_ref,
+    place_hbm,
     home_hbm,
     q,
     keys,
@@ -71,6 +71,7 @@
     lg,
     wts,
     lastg,
+    place,
     local_sem,
     z_sem,
     go_send,
@@ -371,7 +372,9 @@
     lane = iota((QDEV, 128), 1)
     for i, row in enumerate((slot.astype(F32), slot_last.astype(F32), third.astype(F32), weight_ref[...])):
         column = jnp.sum(jnp.where(eye, row, 0.0), axis=1, keepdims=True)
-        place_ref[...] = jnp.where(lane == i, column, 0.0 if i == 0 else place_ref[...])
+        place[...] = jnp.where(lane == i, column, 0.0 if i == 0 else place[...])
+    put_place = pltpu.make_async_copy(place, place_hbm, local_sem.at[6])
+    put_place.start()
     for i in range(3):
         sibling_done(1, i)
     logits(1, y + NY - 2, 5, 2 * BROWS)
@@ -398,6 +401,7 @@
     all_go(0).wait_send()
     all_go(1).wait_send()
 
+    put_place.wait()
     stay_come[0].wait()
     stay_come[1].wait()
     for part in (0, 1):
@@ -405,7 +409,7 @@
         all_come(part).wait_recv()
 
 
-def finish(place_ref, home_hbm, grad_hbm, loss_ref, home, grad, in_sem, out_sem):
+def finish(place_hbm, home_hbm, grad_hbm, loss_ref, place, home, grad, in_sem, out_sem):
     def get(t):
         cols = pl.ds(t * PART, PART) if t < 3 else pl.ds(MAIN, 128)
         return pltpu.make_async_copy(home_hbm.at[:, cols], home.at[:, cols], in_sem.at[t])
@@ -414,10 +418,13 @@
         cols = pl.ds(t * PART, PART)
         return pltpu.make_async_copy(grad.at[:, cols], grad_hbm.at[:, cols], out_sem.at[t])
 
+    get_place = pltpu.make_async_copy(place_hbm, place, in_sem.at[4])
+    get_place.start()
     for t in range(4):
         get(t).start()
-    slot, slot_last, third = [place_ref[:, i : i + 1].astype(jnp.int32) for i in range(3)]
-    weight = place_ref[:, 3:4]
+    get_place.wait()
+    slot, slot_last, third = [place[:, i : i + 1].astype(jnp.int32) for i in range(3)]
+    weight = place[:, 3:4]
     col = iota((QDEV, PIECES * ROWS), 1)
     main = ones_where(slot == col)
     total = None
@@ -452,7 +459,7 @@
             jax.ShapeDtypeStruct(slots, BF),
         ),
         in_specs=[vmem, vmem, vmem, vmem, hbm, hbm],
-        out_specs=(vmem, hbm),
+        out_specs=(hbm, hbm),
         scratch_shapes=[
             pltpu.VMEM((QDEV, D), BF),
             pltpu.VMEM((2, KEYS, D), BF),
@@ -463,7 +470,8 @@
             pltpu.VMEM((PIECES * ROWS, KEYS), F32),
             pltpu.VMEM((PIECES * ROWS, KEYS), BF),
             pltpu.VMEM((COUNT[0], PART), BF),
-            dma((6,)),
+            pltpu.VMEM((QDEV, 128), F32),
+            dma((7,)),
             dma((2, 2)),
             dma((2,)),
             dma((2,)),
@@ -489,12 +497,13 @@
     grad, loss = pl.pallas_call(
         finish,
         out_shape=(jax.ShapeDtypeStruct((QDEV, D), BF), jax.ShapeDtypeStruct((QDEV,), BF)),
-        in_specs=[vmem, hbm],
+        in_specs=[hbm, hbm],
         out_specs=(hbm, vmem),
         scratch_shapes=[
+            pltpu.VMEM((QDEV, 128), F32),
             pltpu.VMEM(slots, BF),
             pltpu.VMEM((QDEV, D), BF),
-            dma((4,)),
+            dma((5,)),
             dma((4,)),
         ],
         compiler_params=pltpu.CompilerParams(vmem_limit_bytes=60 * 1024 * 1024),

time: 123 us -> 121 us (0.984)
  Pallas kernels: 122 us -> 120 us
where the time goes in v4:
time: 121 us
  Pallas kernels  120 us (99%)
    pallas_call x1, Pallas kernels, body(): pl.pallas_call(kernel, out_shape=(jax.ShapeDtypeStruct((QDEV, 128), F32),...  116 us
    pallas_call x1, Pallas kernels, body(): pl.pallas_call(finish, out_shape=(jax.ShapeDtypeStruct((QDEV, D), BF), ja...  4.71 us

profile of v4, /device:TPU:1, one launch (start us, length us, event | category | flops | bytes accessed | tf_op | source)
XLA Modules:
  0.0 120.9 jit_solution(1092032204438677819)
XLA Ops:
  0.6 115.6 %shard_map.77 = (f32[256,128]{1,0:T(8,128)}, bf16[512,2816]{1,0:T(8,128)(2,1)}) custom-call(s32[1,256]{1,0:T(1,128)} %bitcast.5, s32[8,256]{1,0:T(8,128)} %bitcast.4, s32[1,256]{1,0:T(1,128)} %bitcast.6, f32[1,256]{1,0:T(1,128)} %bitcast.7, bf16[256,3584]{1,0:T(8,128)(2,1)} %q_hbm.1, bf16[64,3584]{1,0:T(8,128)(2,1)} %bank_hbm.1), custom_call_target="tpu_custom_call" | custom-call | flops 10000000000 | bytes 10000000 | tf_op jit(solution)/shard_map/pallas_call | solution.py:455
  116.2 4.7 %shard_map.78 = (bf16[256,3584]{1,0:T(8,128)(2,1)}, bf16[256]{0:T(256)(128)(2,1)}) custom-call(f32[256,128]{1,0:T(8,128)} %get-tuple-element.4.place_hbm, bf16[512,2816]{1,0:T(8,128)(2,1)} %get-tuple-element.5.home_hbm), custom_call_target="tpu_custom_call" | custom-call | flops 1000000000 | bytes 5000000 | tf_op jit(solution)/shard_map/pallas_call | solution.py:497
